TPU v7x, 32 devices: a whole 2x2x4 slice. The times are simulated.
32 devices in a mesh: visit: 2 (over x), strip: 16 (over z, y, core).
Axes of the slice: x: 2, y: 2, z: 4, core: 2. Of those that a mesh axis runs over, the one named last changes fastest.
Arguments:
- template: bfloat16 [512, 1024], P('strip', 'visit'), may hold values from -60 to 60
- science_src: bfloat16 [2, 1024, 1024], P('visit', 'strip'), may hold values from -180 to 180
- target_rows: int32 [2, 1024], P('visit'), may hold values from 0 to 511, as said below
- row_taps: bfloat16 [45, 21], replicated, may hold values from -1.25 to 1.25
- col_taps: bfloat16 [45, 21], replicated, may hold values from -1.25 to 1.25
Outputs:
- difference: float32 [2, 512, 1024], P('visit', 'strip')
- kernel_coeffs: float32 [2, 45], P('visit')
Inputs may be any that keep to these rules, and one draw needn't show every extreme that they name: `target_rows`: row j of a visit lies on strip device j // 64; its target's strip is target // 32. Of the 64 rows of one strip device at most 8 target the same strip, and in every visit one strip receives exactly 8 rows from every strip device.
All inputs are finite; a program needn't handle non-finite values.
Results may differ from a plain program's by a relative error of at most 0.0014.
Values may be sent and summed in bfloat16 or wider, within the bound.
A program may use at most 64 MiB of HBM per device.

v0:
```python
import jax
import jax.numpy as jnp
from jax import lax
from jax.sharding import PartitionSpec as P


def with_halo(cells, sides, width):
    for axis, dim in sides:
        count = lax.axis_size(axis)
        ends = count - 1
        head = lax.slice_in_dim(cells, 0, width, axis=dim)
        tail = lax.slice_in_dim(cells, cells.shape[dim] - width, cells.shape[dim], axis=dim)
        cells = jnp.concatenate(
            [
                lax.ppermute(tail, axis, [(i, (i + 1) % count) for i in range(ends)]),
                cells,
                lax.ppermute(head, axis, [((i + 1) % count, i) for i in range(ends)]),
            ],
            axis=dim,
        )
    return cells


def convolve(framed, row_taps, col_taps):
    tap_count = col_taps.shape[1]
    margin = (tap_count - 1) // 2
    basis_count = col_taps.shape[0]
    height = framed.shape[0]
    out_width = framed.shape[1] - 2 * margin
    block_cols = 128
    block_pad = 64
    extra_pad = block_pad - margin
    widened = jnp.pad(framed, ((0, 0), (extra_pad, extra_pad)))
    blocks = out_width // block_cols
    window_cols = block_cols + 2 * block_pad
    pieces = widened.reshape(height, blocks + 1, block_cols)
    windows = jnp.concatenate([pieces[:, :-1], pieces[:, 1:]], axis=2)
    tap_index = jnp.arange(window_cols)[:, None] - jnp.arange(block_cols)[None, :] - extra_pad
    band_table = jnp.zeros((window_cols, basis_count, block_cols), jnp.float32)
    for t in range(tap_count):
        band_table = band_table + jnp.where(
            (tap_index == t)[:, None, :], col_taps[:, t].astype(jnp.float32)[None, :, None], 0.0
        )
    band_table = band_table.astype(jnp.bfloat16).reshape(window_cols, basis_count * block_cols)
    smoothed = jnp.dot(
        windows.reshape(height * blocks, window_cols),
        band_table,
        preferred_element_type=jnp.float32,
    )
    smoothed = smoothed.astype(jnp.bfloat16).reshape(height, blocks, basis_count, block_cols)
    smoothed = jnp.transpose(smoothed, (2, 0, 1, 3)).reshape(basis_count, height, out_width)
    out_rows = height - 2 * margin
    row_lag = jnp.arange(height)[None, :] - jnp.arange(out_rows)[:, None]
    row_band = jnp.zeros((basis_count, out_rows, height), jnp.float32)
    for t in range(tap_count):
        row_band = row_band + jnp.where(
            (row_lag == t)[None, :, :], row_taps[:, t].astype(jnp.float32)[:, None, None], 0.0
        )
    row_band = row_band.astype(jnp.bfloat16)
    basis = jnp.einsum("krs,ksw->krw", row_band, smoothed, preferred_element_type=jnp.float32)
    return basis.astype(jnp.bfloat16)


def split_three(values):
    upper = values.astype(jnp.bfloat16)
    rest = values - upper.astype(jnp.float32)
    middle = rest.astype(jnp.bfloat16)
    lower = (rest - middle.astype(jnp.float32)).astype(jnp.bfloat16)
    return jnp.stack([upper, middle, lower])


def body(template, science_src, target_rows, row_taps, col_taps):
    tap_count = row_taps.shape[1]
    margin = (tap_count - 1) // 2
    basis_count = row_taps.shape[0]
    strips = lax.axis_size("strip")
    visits = lax.axis_size("visit")
    rows_dev = template.shape[0]
    part_width = template.shape[1]
    full_width = part_width * visits
    src_dev = science_src.shape[1]
    capacity = max(2, 2 * src_dev // strips)
    my_strip = lax.axis_index("strip")
    targets = target_rows[0].reshape(strips, src_dev)
    dest_strip = targets // rows_dev
    row_order = jnp.arange(src_dev, dtype=jnp.int32)
    shared_dest = (dest_strip[:, :, None] == dest_strip[:, None, :]) & (
        row_order[:, None] < row_order[None, :]
    )[None]
    arrival = jnp.sum(shared_dest.astype(jnp.int32), axis=1)
    send_slot = dest_strip * capacity + arrival
    my_slots = lax.dynamic_index_in_dim(send_slot, my_strip, 0, keepdims=False)
    slot_ids = jnp.arange(strips * capacity, dtype=jnp.int32)
    placer = (my_slots[None, :] == slot_ids[:, None]).astype(jnp.bfloat16)
    outgoing = jnp.dot(placer, science_src[0], preferred_element_type=jnp.float32).astype(
        jnp.bfloat16
    )
    outgoing = outgoing.reshape(strips, capacity, full_width)
    incoming = lax.all_to_all(outgoing, "strip", split_axis=0, concat_axis=0, tiled=True)
    anchor = (jnp.arange(strips, dtype=jnp.int32) * capacity)[:, None] + arrival
    aimed_here = dest_strip == my_strip
    local_row = targets - my_strip * rows_dev
    slot_hit = (aimed_here[..., None] & (anchor[..., None] == slot_ids)).reshape(
        strips * src_dev, strips * capacity
    )
    row_hit = (local_row[..., None] == jnp.arange(rows_dev, dtype=jnp.int32)).reshape(
        strips * src_dev, rows_dev
    )
    spread = lax.dot_general(
        row_hit.astype(jnp.bfloat16),
        slot_hit.astype(jnp.bfloat16),
        (((0,), (0,)), ((), ())),
        preferred_element_type=jnp.float32,
    )
    spread = spread.astype(jnp.bfloat16)
    science = jnp.dot(
        spread, incoming.reshape(strips * capacity, full_width), preferred_element_type=jnp.float32
    )
    rimmed = with_halo(template, (("strip", 0),), margin)
    gathered = lax.all_gather(rimmed, "visit", axis=1, tiled=True)
    framed = jnp.pad(gathered, ((0, 0), (margin, margin)))
    basis = convolve(framed, row_taps, col_taps)
    basis_flat = basis.reshape(basis_count, rows_dev * full_width)
    science_parts = split_three(science.reshape(rows_dev * full_width))
    moment_parts = lax.dot_general(
        science_parts, basis_flat, (((1,), (1,)), ((), ())), preferred_element_type=jnp.float32
    )
    moment_part = jnp.sum(moment_parts, axis=0)
    gram_part = lax.dot_general(
        basis_flat, basis_flat, (((1,), (1,)), ((), ())), preferred_element_type=jnp.float32
    )
    gram_total, moment = lax.psum((gram_part, moment_part), "strip")
    factor = jnp.linalg.cholesky(gram_total)
    forward = lax.linalg.triangular_solve(factor, moment[:, None], left_side=True, lower=True)
    answer = lax.linalg.triangular_solve(
        factor, forward, left_side=True, lower=True, transpose_a=True
    )
    kernel_coeffs = answer[:, 0]
    coeff_parts = split_three(kernel_coeffs)
    model_parts = jnp.dot(coeff_parts, basis_flat, preferred_element_type=jnp.float32)
    model = jnp.sum(model_parts, axis=0).reshape(rows_dev, full_width)
    difference = science - model
    return (difference[None], kernel_coeffs[None])


def solution(mesh):
    in_specs = (P("strip", "visit"), P("visit", "strip", None), P("visit", None), P(), P())
    out_specs = (P("visit", "strip", None), P("visit", None))
    return jax.shard_map(body, mesh=mesh, in_specs=in_specs, out_specs=out_specs, check_vma=False)
```

profile of v0, /device:TPU:0, one launch (start us, length us, event | category | flops | bytes accessed | tf_op | source)
XLA Modules:
  0.0 161.6 jit_solution(15151071377649270100)
XLA Ops:
  0.6 0.0 copy-start
  0.6 1.4 fusion.140
  2.0 2.3 %collective-permute-start = (bf16[10,512]{1,0:T(8,128)(2,1)}, bf16[10,512]{1,0:T(8,128)(2,1)S(1)}, u32[]{:S(2)}, u32[]{:S(2)}) collective-permute-start(bf16[10,512]{1,0:T(8,128)(2,1)} %get-tuple-element.10), channel_id=1, source_target_pairs={{0,1},{1,2},{2,3},{3,4},{4,5},{5,6},{6,7},{7,8},{8,9},{9,10},{10,1... | collective-permute-start | bytes 30728 | tf_op jit(solution)/shard_map/ppermute | solution.py:15
  4.4 1.3 collective-permute-start.1
  5.7 0.5 broadcast.1383
  6.2 1.3 reduce.9
  7.6 0.1 reshape_squeeze.3
  7.6 0.6 broadcast_compare_fusion
  8.2 0.2 convert_reduce_fusion
  8.5 0.0 copy-done
  8.5 0.9 fusion.8
  9.4 9.4 %all-to-all-start = ((bf16[16,8,1024]{2,1,0:T(8,128)(2,1)}), bf16[16,8,1024]{2,1,0:T(8,128)(2,1)}, u32[]{:S(2)}, u32[]{:S(2)}) async-start(bf16[16,8,1024]{2,1,0:T(8,128)(2,1)} %fusion.8), calls=%async_computation | async-start | bytes 524288 | tf_op jit(solution)/shard_map/all_to_all | solution.py:99
  19.0 0.7 fusion.87
  19.7 0.6 fusion.89
  20.3 0.7 fusion.91
  21.0 1.6 %bitcast_convert_fusion.20 = (f32[45]{0:T(128)}, f32[45]{0:T(128)}, f32[45]{0:T(128)}, f32[45]{0:T(128)}, f32[45]{0:T(128)}, /*index=5*/f32[45]{0:T(128)}, f32[4...) fusion(bf16[45,21]{0,1:T(8,128)(2,1)} %param.9), kind=kLoop, calls=%fused_computation.179 | loop fusion | flops 855 | bytes 5130 | tf_op jit(solution)/shard_map/convert_element_type | solution.py:42
  22.6 1.3 bitcast_convert_fusion.1
  23.9 0.6 fusion.93
  24.6 0.6 fusion.102
  25.2 0.6 fusion.104
  25.8 0.6 fusion.106
  26.4 0.6 fusion.108
  27.0 0.6 fusion.110
  27.6 0.6 fusion.112
  28.2 0.6 fusion.114
  28.8 0.6 fusion.116
  29.4 0.6 fusion.118
  30.0 0.6 fusion.120
  30.6 1.7 %bitcast_convert_fusion.41 = (f32[45]{0:T(128)}, f32[45]{0:T(128)}, f32[45]{0:T(128)}, f32[45]{0:T(128)}, f32[45]{0:T(128)}, /*index=5*/f32[45]{0:T(128)}, f32[4...) fusion(bf16[45,21]{0,1:T(8,128)(2,1)} %param.8), kind=kLoop, calls=%fused_computation.200 | loop fusion | flops 855 | bytes 5130 | tf_op jit(solution)/shard_map/convert_element_type | solution.py:57
  32.3 1.3 bitcast_convert_fusion.22
  33.6 0.7 broadcast_add_fusion
  34.3 11.5 %add_convert_fusion = bf16[256,45,128]{0,2,1:T(8,128)(2,1)S(1)} fusion(f32[45]{0:T(128)} %get-tuple-element.53, f32[45]{0:T(128)} %get-tuple-element.52, f32[45]{0:T(128)} %get-tuple-element.34, f32[45]{0:T(128)} %get-tuple-element.35, f32[45]{0:T(128)} %get-tuple-element.36, f32[45]{0:T(128)} %get-tuple-element.37, f32[45]{0:T(128)} %get-tuple-element.38, ...), kind=kLoop, calls=%fused_computation.1 | loop fusion | flops 61931520 | bytes 3641028 | tf_op jit(solution)/shard_map/convert_element_type | solution.py:44
  45.8 0.8 fusion.122
  46.6 0.0 collective-permute-done
  46.6 0.0 collective-permute-done.1
  46.6 0.8 pad_maximum_fusion
  47.4 4.9 %all_gather.3 = bf16[52,1024]{1,0:T(8,128)(2,1)S(1)} all-gather(bf16[52,512]{1,0:T(8,128)(2,1)S(1)} %pad_maximum_fusion), channel_id=1, replica_groups=mesh['visit'=2,'strip'=16] {'visit'}, dimensions={1}, use_global_device_ids=true | all-gather | bytes 159744 | tf_op jit(solution)/shard_map/all_gather | solution.py:120
  52.2 0.1 pad.21
  52.3 0.1 reshape.1496
  52.5 3.7 %fusion.4 = bf16[45,52,8,128]{3,2,0,1:T(8,128)(2,1)} fusion(bf16[256,5760]{0,1:T(8,128)(2,1)S(1)} %bitcast.207, bf16[52,8,128]{2,1,0:T(8,128)(2,1)S(1)} %get-tuple-element.7, bf16[52,8,128]{2,1,0:T(8,128)(2,1)S(1)} %get-tuple-element.6), kind=kOutput, calls=%fused_computation.6 | convolution fusion | flops 1229656064 | bytes 7954432 | tf_op jit(solution)/shard_map/dot_general | solution.py:45
  56.4 0.0 copy-start.23
  56.6 8.5 %reshape.1499 = bf16[45,52,1024]{2,0,1:T(8,128)(2,1)} reshape(bf16[45,52,8,128]{3,2,0,1:T(8,128)(2,1)} %fusion.4) | data formatting | bytes 9584640 | tf_op jit(solution)/shard_map/reshape | solution.py:51
  65.1 0.0 copy-done.3
  65.1 0.0 copy-done.5
  65.5 13.3 %fusion.5 = bf16[45,32,1024]{2,1,0:T(8,128)(2,1)S(1)} fusion(bf16[45,52,1024]{2,0,1:T(8,128)(2,1)} %reshape.1499, f32[45]{0:T(128)} %get-tuple-element.32, f32[45]{0:T(128)} %get-tuple-element.31, f32[45]{0:T(128)S(1)} %copy-done.26, f32[45]{0:T(128)S(1)} %copy-done.27, f32[45]{0:T(128)S(1)} %copy-done.28, f32[45]{0:T(128)S(1)} %copy-done.29, ...), kind=kOutput, calls=%fused_computation.7 | convolution fusion | flops 157973760 | bytes 7780164 | tf_op jit(solution)/shard_map/krs,ksw->krw/dot_general | solution.py:60
  78.8 0.5 pad.22
  79.3 1.9 %copy.25 = bf16[6,8,32,1024]{3,1,2,0:T(8,128)(2,1)S(1)} copy(bf16[6,8,32,1024]{3,2,1,0:T(8,128)(2,1)S(1)} %bitcast.206) | data formatting | bytes 6291456
  81.2 6.1 %fusion.9 = f32[45,45]{0,1:T(8,128)S(1)} fusion(bf16[45,32,1024]{2,1,0:T(8,128)(2,1)S(1)} %fusion.5), kind=kOutput, calls=%fused_computation.11 | convolution fusion | flops 132710400 | bytes 2957220 | tf_op jit(solution)/shard_map/dot_general | solution.py:129
  87.3 0.0 all-to-all-done
  87.4 1.6 fusion.13
  88.9 0.1 copy.24
  89.1 0.2 fusion.125
  89.2 0.1 convert_element_type.631
  89.3 1.0 convolution_reduce_fusion.1
  90.3 60.7 %all-reduce.2 = (f32[45,45]{0,1:T(8,128)S(1)}, f32[45]{0:T(128)S(1)}) all-reduce(f32[45,45]{0,1:T(8,128)S(1)} %fusion.9, f32[45]{0:T(128)S(1)} %convolution_reduce_fusion.1), channel_id=1, replica_groups=mesh['visit'=2,'strip'=16] {'strip'}, use_global_device_ids=true, to_apply=%region_1.2 | all-reduce | flops 2070 | bytes 16560 | tf_op jit(solution)/shard_map/psum | solution.py:132
  151.0 0.1 copy.21
  151.1 4.1 %cholesky.16 = f32[45,45]{1,0:T(8,128)S(1)} custom-call(f32[45,45]{1,0:T(8,128)S(1)} %fusion.101), custom_call_target="Cholesky" | custom-call | tf_op jit(solution)/shard_map/jit(cholesky)/cholesky | solution.py:133
  155.2 0.6 compare_reduce_fusion
  155.9 0.7 fusion.97
  156.5 3.4 %custom-call.8 = f32[1,45,45]{1,2,0:T(8,128)S(1)} custom-call(f32[1,45,45]{2,1,0:T(8,128)S(1)} %fusion.97), custom_call_target="InvertDiagBlocksLowerTriangular" | custom-call | tf_op jit(solution)/shard_map/triangular_solve | solution.py:135
  160.0 0.2 convolution_bitcast_fusion.1
  160.1 0.2 fusion.98
  160.3 0.6 convolution_reduce_fusion
  160.9 0.7 subtract_bitcast_fusion
  (101 shorter events, 0.6 us)
Async XLA Ops:
  0.6 7.9 %copy-start = (bf16[1,64,1024]{2,1,0:T(8,128)(2,1)S(1)}, bf16[1,64,1024]{2,1,0:T(8,128)(2,1)}, u32[]{:S(2)}) copy-start(bf16[1,64,1024]{2,1,0:T(8,128)(2,1)} %param.6) | copy-start | bytes 393220
  2.0 44.5 %collective-permute-start = (bf16[10,512]{1,0:T(8,128)(2,1)}, bf16[10,512]{1,0:T(8,128)(2,1)S(1)}, u32[]{:S(2)}, u32[]{:S(2)}) collective-permute-start(bf16[10,512]{1,0:T(8,128)(2,1)} %get-tuple-element.10), channel_id=1, source_target_pairs={{0,1},{1,2},{2,3},{3,4},{4,5},{5,6},{6,7},{7,8},{8,9},{9,10},{10,1... | collective-permute-start | bytes 30728 | tf_op jit(solution)/shard_map/ppermute | solution.py:15
  4.4 42.2 %collective-permute-start.1 = (bf16[10,512]{1,0:T(8,128)(2,1)}, bf16[10,512]{1,0:T(8,128)(2,1)}, u32[]{:S(2)}, u32[]{:S(2)}) collective-permute-start(bf16[10,512]{1,0:T(8,128)(2,1)} %get-tuple-element.11), channel_id=1, source_target_pairs={{1,0},{2,1},{3,2},{4,3},{5,4},{6,5},{7,6},{8,7},{9,8},{10,9},{11,1... | collective-permute-start | bytes 30728 | tf_op jit(solution)/shard_map/ppermute | solution.py:17
  9.4 77.9 %all-to-all-start = ((bf16[16,8,1024]{2,1,0:T(8,128)(2,1)}), bf16[16,8,1024]{2,1,0:T(8,128)(2,1)}, u32[]{:S(2)}, u32[]{:S(2)}) async-start(bf16[16,8,1024]{2,1,0:T(8,128)(2,1)} %fusion.8), calls=%async_computation | async-start | bytes 524288 | tf_op jit(solution)/shard_map/all_to_all | solution.py:99
  56.2 8.9 %copy-start.3 = (pred[32,52]{1,0:T(8,128)(4,1)S(1)}, pred[32,52]{1,0:T(8,128)(4,1)}, u32[]{:S(2)}) copy-start(pred[32,52]{1,0:T(8,128)(4,1)} %get-tuple-element.78) | copy-start | bytes 4996
  56.2 8.9 %copy-start.4 = (pred[32,52]{1,0:T(8,128)(4,1)S(1)}, pred[32,52]{1,0:T(8,128)(4,1)}, u32[]{:S(2)}) copy-start(pred[32,52]{1,0:T(8,128)(4,1)} %get-tuple-element.79) | copy-start | bytes 4996
  56.2 8.9 %copy-start.5 = (pred[32,52]{1,0:T(8,128)(4,1)S(1)}, pred[32,52]{1,0:T(8,128)(4,1)}, u32[]{:S(2)}) copy-start(pred[32,52]{1,0:T(8,128)(4,1)} %get-tuple-element.80) | copy-start | bytes 4996
  56.2 8.9 %copy-start.6 = (pred[32,52]{1,0:T(8,128)(4,1)S(1)}, pred[32,52]{1,0:T(8,128)(4,1)}, u32[]{:S(2)}) copy-start(pred[32,52]{1,0:T(8,128)(4,1)} %get-tuple-element.81) | copy-start | bytes 4996
  56.2 8.9 %copy-start.7 = (pred[32,52]{1,0:T(8,128)(4,1)S(1)}, pred[32,52]{1,0:T(8,128)(4,1)}, u32[]{:S(2)}) copy-start(pred[32,52]{1,0:T(8,128)(4,1)} %get-tuple-element.82) | copy-start | bytes 4996
  56.2 8.9 %copy-start.8 = (pred[32,52]{1,0:T(8,128)(4,1)S(1)}, pred[32,52]{1,0:T(8,128)(4,1)}, u32[]{:S(2)}) copy-start(pred[32,52]{1,0:T(8,128)(4,1)} %get-tuple-element.83) | copy-start | bytes 4996
  56.2 8.9 %copy-start.9 = (pred[32,52]{1,0:T(8,128)(4,1)S(1)}, pred[32,52]{1,0:T(8,128)(4,1)}, u32[]{:S(2)}) copy-start(pred[32,52]{1,0:T(8,128)(4,1)} %get-tuple-element.84) | copy-start | bytes 4996
  56.2 8.9 %copy-start.10 = (pred[32,52]{1,0:T(8,128)(4,1)S(1)}, pred[32,52]{1,0:T(8,128)(4,1)}, u32[]{:S(2)}) copy-start(pred[32,52]{1,0:T(8,128)(4,1)} %get-tuple-element.85) | copy-start | bytes 4996
  56.3 8.9 %copy-start.11 = (pred[32,52]{1,0:T(8,128)(4,1)S(1)}, pred[32,52]{1,0:T(8,128)(4,1)}, u32[]{:S(2)}) copy-start(pred[32,52]{1,0:T(8,128)(4,1)} %get-tuple-element.86) | copy-start | bytes 4996
  56.3 8.9 %copy-start.12 = (pred[32,52]{1,0:T(8,128)(4,1)S(1)}, pred[32,52]{1,0:T(8,128)(4,1)}, u32[]{:S(2)}) copy-start(pred[32,52]{1,0:T(8,128)(4,1)} %get-tuple-element.87) | copy-start | bytes 4996
  56.3 8.9 %copy-start.13 = (pred[32,52]{1,0:T(8,128)(4,1)S(1)}, pred[32,52]{1,0:T(8,128)(4,1)}, u32[]{:S(2)}) copy-start(pred[32,52]{1,0:T(8,128)(4,1)} %get-tuple-element.88) | copy-start | bytes 4996
  56.3 8.9 %copy-start.14 = (pred[32,52]{1,0:T(8,128)(4,1)S(1)}, pred[32,52]{1,0:T(8,128)(4,1)}, u32[]{:S(2)}) copy-start(pred[32,52]{1,0:T(8,128)(4,1)} %get-tuple-element.89) | copy-start | bytes 4996
  56.3 8.9 %copy-start.15 = (pred[32,52]{1,0:T(8,128)(4,1)S(1)}, pred[32,52]{1,0:T(8,128)(4,1)}, u32[]{:S(2)}) copy-start(pred[32,52]{1,0:T(8,128)(4,1)} %get-tuple-element.90) | copy-start | bytes 4996
  56.3 8.9 %copy-start.16 = (pred[32,52]{1,0:T(8,128)(4,1)S(1)}, pred[32,52]{1,0:T(8,128)(4,1)}, u32[]{:S(2)}) copy-start(pred[32,52]{1,0:T(8,128)(4,1)} %get-tuple-element.91) | copy-start | bytes 4996
  56.3 8.9 %copy-start.17 = (pred[32,52]{1,0:T(8,128)(4,1)S(1)}, pred[32,52]{1,0:T(8,128)(4,1)}, u32[]{:S(2)}) copy-start(pred[32,52]{1,0:T(8,128)(4,1)} %get-tuple-element.92) | copy-start | bytes 4996
  56.3 8.9 %copy-start.18 = (pred[32,52]{1,0:T(8,128)(4,1)S(1)}, pred[32,52]{1,0:T(8,128)(4,1)}, u32[]{:S(2)}) copy-start(pred[32,52]{1,0:T(8,128)(4,1)} %get-tuple-element.93) | copy-start | bytes 4996
  56.3 8.9 %copy-start.19 = (pred[32,52]{1,0:T(8,128)(4,1)S(1)}, pred[32,52]{1,0:T(8,128)(4,1)}, u32[]{:S(2)}) copy-start(pred[32,52]{1,0:T(8,128)(4,1)} %get-tuple-element.94) | copy-start | bytes 4996
  56.3 8.9 %copy-start.20 = (pred[32,52]{1,0:T(8,128)(4,1)S(1)}, pred[32,52]{1,0:T(8,128)(4,1)}, u32[]{:S(2)}) copy-start(pred[32,52]{1,0:T(8,128)(4,1)} %get-tuple-element.95) | copy-start | bytes 4996
  56.4 8.9 %copy-start.21 = (pred[32,52]{1,0:T(8,128)(4,1)S(1)}, pred[32,52]{1,0:T(8,128)(4,1)}, u32[]{:S(2)}) copy-start(pred[32,52]{1,0:T(8,128)(4,1)} %get-tuple-element.96) | copy-start | bytes 4996
  56.4 8.9 %copy-start.22 = (pred[32,52]{1,0:T(8,128)(4,1)S(1)}, pred[32,52]{1,0:T(8,128)(4,1)}, u32[]{:S(2)}) copy-start(pred[32,52]{1,0:T(8,128)(4,1)} %get-tuple-element.97) | copy-start | bytes 4996
  56.4 8.9 %copy-start.23 = (pred[32,52]{1,0:T(8,128)(4,1)S(1)}, pred[32,52]{1,0:T(8,128)(4,1)}, u32[]{:S(2)}) copy-start(pred[32,52]{1,0:T(8,128)(4,1)} %fusion.122) | copy-start | bytes 4996
  56.4 8.9 %copy-start.25 = (f32[45]{0:T(128)S(1)}, f32[45]{0:T(128)}, u32[]{:S(2)}) copy-start(f32[45]{0:T(128)} %get-tuple-element.12) | copy-start | bytes 544
  56.4 8.9 %copy-start.26 = (f32[45]{0:T(128)S(1)}, f32[45]{0:T(128)}, u32[]{:S(2)}) copy-start(f32[45]{0:T(128)} %get-tuple-element.13) | copy-start | bytes 544
  56.4 8.9 %copy-start.27 = (f32[45]{0:T(128)S(1)}, f32[45]{0:T(128)}, u32[]{:S(2)}) copy-start(f32[45]{0:T(128)} %get-tuple-element.14) | copy-start | bytes 544
  56.4 8.9 %copy-start.28 = (f32[45]{0:T(128)S(1)}, f32[45]{0:T(128)}, u32[]{:S(2)}) copy-start(f32[45]{0:T(128)} %get-tuple-element.15) | copy-start | bytes 544
  56.4 8.9 %copy-start.29 = (f32[45]{0:T(128)S(1)}, f32[45]{0:T(128)}, u32[]{:S(2)}) copy-start(f32[45]{0:T(128)} %get-tuple-element.16) | copy-start | bytes 544
  56.4 8.9 %copy-start.30 = (f32[45]{0:T(128)S(1)}, f32[45]{0:T(128)}, u32[]{:S(2)}) copy-start(f32[45]{0:T(128)} %get-tuple-element.17) | copy-start | bytes 544
  56.5 8.9 %copy-start.31 = (f32[45]{0:T(128)S(1)}, f32[45]{0:T(128)}, u32[]{:S(2)}) copy-start(f32[45]{0:T(128)} %get-tuple-element.18) | copy-start | bytes 544
  56.5 8.9 %copy-start.32 = (f32[45]{0:T(128)S(1)}, f32[45]{0:T(128)}, u32[]{:S(2)}) copy-start(f32[45]{0:T(128)} %get-tuple-element.19) | copy-start | bytes 544
  56.5 8.9 %copy-start.33 = (f32[45]{0:T(128)S(1)}, f32[45]{0:T(128)}, u32[]{:S(2)}) copy-start(f32[45]{0:T(128)} %get-tuple-element.20) | copy-start | bytes 544
  56.5 8.9 %copy-start.34 = (f32[45]{0:T(128)S(1)}, f32[45]{0:T(128)}, u32[]{:S(2)}) copy-start(f32[45]{0:T(128)} %get-tuple-element.21) | copy-start | bytes 544
  56.5 8.9 %copy-start.35 = (f32[45]{0:T(128)S(1)}, f32[45]{0:T(128)}, u32[]{:S(2)}) copy-start(f32[45]{0:T(128)} %get-tuple-element.22) | copy-start | bytes 544
  56.5 8.9 %copy-start.36 = (f32[45]{0:T(128)S(1)}, f32[45]{0:T(128)}, u32[]{:S(2)}) copy-start(f32[45]{0:T(128)} %get-tuple-element.23) | copy-start | bytes 544
  56.5 8.9 %copy-start.37 = (f32[45]{0:T(128)S(1)}, f32[45]{0:T(128)}, u32[]{:S(2)}) copy-start(f32[45]{0:T(128)} %get-tuple-element.24) | copy-start | bytes 544
  56.5 8.9 %copy-start.38 = (f32[45]{0:T(128)S(1)}, f32[45]{0:T(128)}, u32[]{:S(2)}) copy-start(f32[45]{0:T(128)} %get-tuple-element.25) | copy-start | bytes 544
  56.5 8.9 %copy-start.39 = (f32[45]{0:T(128)S(1)}, f32[45]{0:T(128)}, u32[]{:S(2)}) copy-start(f32[45]{0:T(128)} %get-tuple-element.26) | copy-start | bytes 544
  56.5 8.9 %copy-start.40 = (f32[45]{0:T(128)S(1)}, f32[45]{0:T(128)}, u32[]{:S(2)}) copy-start(f32[45]{0:T(128)} %get-tuple-element.27) | copy-start | bytes 544
  56.6 8.9 %copy-start.41 = (f32[45]{0:T(128)S(1)}, f32[45]{0:T(128)}, u32[]{:S(2)}) copy-start(f32[45]{0:T(128)} %get-tuple-element.28) | copy-start | bytes 544
  56.6 8.9 %copy-start.42 = (f32[45]{0:T(128)S(1)}, f32[45]{0:T(128)}, u32[]{:S(2)}) copy-start(f32[45]{0:T(128)} %get-tuple-element.29) | copy-start | bytes 544
  56.6 8.9 %copy-start.43 = (f32[45]{0:T(128)S(1)}, f32[45]{0:T(128)}, u32[]{:S(2)}) copy-start(f32[45]{0:T(128)} %get-tuple-element.30) | copy-start | bytes 544
  79.3 8.1 %copy-start.1 = (s32[16,64]{1,0:T(8,128)S(1)}, s32[16,64]{1,0:T(8,128)}, u32[]{:S(2)}) copy-start(s32[16,64]{1,0:T(8,128)} %get-tuple-element.56) | copy-start | bytes 12292
  79.3 8.1 %copy-start.2 = (s32[16,64]{1,0:T(8,128)S(1)}, s32[16,64]{1,0:T(8,128)}, u32[]{:S(2)}) copy-start(s32[16,64]{1,0:T(8,128)} %get-tuple-element.57) | copy-start | bytes 12292
  79.3 8.1 %copy-start.24 = (pred[16,64]{1,0:T(8,128)(4,1)S(1)}, pred[16,64]{1,0:T(8,128)(4,1)}, u32[]{:S(2)}) copy-start(pred[16,64]{1,0:T(8,128)(4,1)} %get-tuple-element.4) | copy-start | bytes 3076
  160.3 1.3 copy-start.44
where the time goes:
time: 162 us
  blocking collectives  65.5 us (40%)
  other arithmetic  40.5 us (25%)
  matrix products  27.5 us (17%)
  local copies, waits for them, and re-layouts  13.5 us (8%)
  starting transfers between devices  13 us (8%)
    psum x1, blocking collectives, body(): gram_total, moment = lax.psum((gram_part, moment_part), 'strip')  60.7 us
    dot_general x1, matrix products, convolve(): jnp.einsum('krs,ksw->krw', row_band, smoothed, preferred_element_type=jnp...  13.3 us
    convert_element_type x1, other arithmetic, convolve(): band_table.astype(jnp.bfloat16)  11.5 us
    all_to_all x1, starting transfers between devices, body(): lax.all_to_all(outgoing, 'strip', split_axis=0, concat_axis=0, tiled=True)  9.35 us
    reshape x1, local copies, waits for them, and re-layouts, convolve(): jnp.transpose(smoothed, (2, 0, 1, 3))  8.52 us
    eq x11, other arithmetic, convolve(): row_lag == t  6.85 us
    dot_general x1, matrix products, body(): lax.dot_general(basis_flat, basis_flat, (((1,), (1,)), ((), ())), preferr...  6.14 us
    all_gather x1, blocking collectives, body(): gathered = lax.all_gather(rimmed, 'visit', axis=1, tiled=True)  4.85 us
  transfers between devices with their start and end apart: 3, of which 0 were waited for; matrix products, arithmetic and copies ran while one was open for 41% of the time, Pallas kernels for 0%

commit v1 on v0

v1 whole, which is shorter than its diff:
```python
import functools
import math

import jax
import jax.numpy as jnp
from jax import lax
from jax.experimental import pallas as pl
from jax.experimental.pallas import tpu as pltpu
from jax.sharding import PartitionSpec as P

MESH = pl.DeviceIdType.MESH
F32 = jnp.float32
BF16 = jnp.bfloat16
LANES = 128
GROUP = 8
TILE = 16


def split_three(values):
    upper = values.astype(BF16).astype(F32)
    rest = values - upper
    middle = rest.astype(BF16).astype(F32)
    return upper, middle, rest - middle


def fit_kernel(
    dims,
    tmpl_ref, src_ref, place_ref, spread_ref, row_ref, col_ref,
    diff_ref, coef_ref,
    frame, outbox, inbox, wide, taps_pad, lag, band, rowband, sm, images, low_buf, high_buf,
    t_send, t_recv, s_send, s_recv, low_send, low_recv, high_send, high_recv,
):
    visits, strips, capacity, low, high = dims
    v = lax.axis_index("visit")
    me = lax.axis_index("strip")
    rows, width = tmpl_ref.shape
    cols = width * visits
    basis_count, taps = row_ref.shape
    margin = (taps - 1) // 2
    padded = images.shape[1]
    height = frame.shape[0]
    fold = TILE // capacity
    piece = cols // fold
    blocks = cols // LANES
    window = 2 * LANES
    lead = LANES // 2

    barrier = pltpu.get_barrier_semaphore()
    for off in range(1, strips):
        pl.semaphore_signal(
            barrier, inc=1, device_id=(v, lax.rem(me + off, strips)), device_id_type=MESH
        )
    for off in range(1, visits):
        other = lax.rem(v + off, visits)
        pl.semaphore_signal(barrier, inc=1, device_id=(other, me), device_id_type=MESH)

        @pl.when(me > 0)
        def _():
            pl.semaphore_signal(barrier, inc=1, device_id=(other, me - 1), device_id_type=MESH)

        @pl.when(me < strips - 1)
        def _():
            pl.semaphore_signal(barrier, inc=1, device_id=(other, me + 1), device_id_type=MESH)

    slot = lax.broadcasted_iota(jnp.int32, (strips * TILE, src_ref.shape[0]), 0)
    packed = jnp.zeros((strips * TILE, piece), F32)
    for f in range(fold):
        hit = (slot == place_ref[...] + f * capacity).astype(F32).astype(BF16)
        packed += jnp.dot(
            hit, src_ref[:, f * piece : (f + 1) * piece], preferred_element_type=F32
        )
    outbox[...] = packed.astype(BF16).reshape(strips, TILE, piece)

    neighbours = jnp.where(me > 0, 1, 0) + jnp.where(me < strips - 1, 1, 0)
    pl.semaphore_wait(barrier, strips - 1 + (visits - 1) * (1 + neighbours))

    def span(u):
        return pl.ds(pl.multiple_of(u * width, width), width)

    def main_copy(owner, to):
        return pltpu.make_async_remote_copy(
            src_ref=tmpl_ref, dst_ref=frame.at[pl.ds(TILE, rows), span(owner)],
            send_sem=t_send.at[0, to], recv_sem=t_recv.at[0, owner],
            device_id=(to, me), device_id_type=MESH,
        )

    def down_copy(owner, to, strip):
        return pltpu.make_async_remote_copy(
            src_ref=tmpl_ref.at[pl.ds(rows - TILE, TILE), :],
            dst_ref=frame.at[pl.ds(0, TILE), span(owner)],
            send_sem=t_send.at[1, to], recv_sem=t_recv.at[1, owner],
            device_id=(to, strip), device_id_type=MESH,
        )

    def up_copy(owner, to, strip):
        return pltpu.make_async_remote_copy(
            src_ref=tmpl_ref.at[pl.ds(0, TILE), :],
            dst_ref=frame.at[pl.ds(TILE + rows, TILE), span(owner)],
            send_sem=t_send.at[2, to], recv_sem=t_recv.at[2, owner],
            device_id=(to, strip), device_id_type=MESH,
        )

    for off in range(visits):
        to = lax.rem(v + off, visits)
        if off:
            main_copy(v, to).start()

        @pl.when(me < strips - 1)
        def _():
            down_copy(v, to, me + 1).start()

        @pl.when(me > 0)
        def _():
            up_copy(v, to, me - 1).start()

    def row_copy(off):
        to = lax.rem(me + off, strips)
        return pltpu.make_async_remote_copy(
            src_ref=outbox.at[to], dst_ref=inbox.at[me],
            send_sem=s_send.at[to], recv_sem=s_recv.at[me],
            device_id=(v, to), device_id_type=MESH,
        )

    for off in range(1, strips):
        row_copy(off).start()

    inbox[me] = outbox[me]
    frame[pl.ds(TILE, rows), span(v)] = tmpl_ref[...]

    @pl.when(me == 0)
    def _():
        frame[pl.ds(0, TILE), :] = jnp.zeros((TILE, cols), BF16)

    @pl.when(me == strips - 1)
    def _():
        frame[pl.ds(TILE + rows, TILE), :] = jnp.zeros((TILE, cols), BF16)

    shift = lead - margin
    taps_pad[...] = jnp.zeros(taps_pad.shape, F32)
    taps_pad[0, 0:basis_count, 0:taps] = col_ref[...].astype(F32)
    taps_pad[1, 0:basis_count, 0:taps] = row_ref[...].astype(F32)
    square = (LANES, LANES)
    turn = (
        lax.broadcasted_iota(jnp.int32, square, 0) + lax.broadcasted_iota(jnp.int32, square, 1)
        == LANES - shift
    ).astype(F32).astype(BF16)
    reverse = jnp.dot(taps_pad[0].astype(BF16), turn, preferred_element_type=F32)
    for j in range(TILE):
        lag[:, j, :] = pltpu.roll(reverse, j, 1) if j else reverse
    tile_row = lax.broadcasted_iota(jnp.int32, (TILE, LANES), 0)
    tile_col = lax.broadcasted_iota(jnp.int32, (TILE, LANES), 1)
    for i in range(window // TILE):
        gap = i * TILE + tile_row - tile_col - shift
        keep = (gap >= 0) & (gap < taps)
        turned = (i * TILE) % LANES
        for k in range(padded):
            entry = pltpu.roll(lag[k], turned, 1) if turned else lag[k]
            band[i * TILE : (i + 1) * TILE, k * LANES : (k + 1) * LANES] = jnp.where(
                keep, entry, 0.0
            ).astype(BF16)

    line = lax.broadcasted_iota(jnp.int32, (GROUP, LANES), 0)
    per_tile = LANES // height
    for g in range(padded // GROUP):
        base = pltpu.roll(taps_pad[1, g * GROUP : (g + 1) * GROUP, :], TILE - margin, 1)
        parts = []
        for q in range(GROUP // per_tile):
            part = jnp.zeros((GROUP, LANES), F32)
            for e in range(per_tile):
                moved = pltpu.roll(base, e * height, 1) if e else base
                part = jnp.where(line == q * per_tile + e, moved, part)
            parts.append(part)
        for r in range(0, rows, 2):
            pair = []
            for d in (r, r + 1):
                pair.append(
                    jnp.concatenate([pltpu.roll(p, d, 1) if d else p for p in parts], axis=1)
                )
            rowband[g, r * GROUP : (r + 2) * GROUP, :] = jnp.concatenate(pair, axis=0).astype(BF16)

    for off in range(1, visits):
        main_copy(lax.rem(v + off, visits), v).wait_recv()
    for off in range(visits):
        owner = lax.rem(v + off, visits)

        @pl.when(me > 0)
        def _():
            down_copy(owner, v, me).wait_recv()

        @pl.when(me < strips - 1)
        def _():
            up_copy(owner, v, me).wait_recv()

    full = jnp.concatenate(
        [frame[...].astype(F32), jnp.zeros((height, LANES), F32)], axis=1
    )
    shifted = pltpu.roll(full, lead, 1).astype(BF16)
    for b in range(blocks):
        wide[b * height : (b + 1) * height, :] = shifted[:, b * LANES : b * LANES + window]

    def group_image(g):
        span_g = GROUP * LANES
        out = jnp.dot(
            wide[...], band[:, g * span_g : (g + 1) * span_g], preferred_element_type=F32
        ).astype(BF16)
        for b in range(blocks):
            for k in range(GROUP):
                sm[g % 2, k * height : (k + 1) * height, b * LANES : (b + 1) * LANES] = out[
                    b * height : (b + 1) * height, k * LANES : (k + 1) * LANES
                ]
        return jnp.dot(rowband[g], sm[g % 2], preferred_element_type=F32)

    def put(pair, first, second):
        images[:, pair * TILE : (pair + 1) * TILE, :] = jnp.concatenate(
            [first.reshape(rows, GROUP, cols), second.reshape(rows, GROUP, cols)], axis=1
        ).astype(BF16)

    pairs = padded // TILE
    for pair in range(pairs - 1):
        put(pair, group_image(2 * pair), group_image(2 * pair + 1))
    first, second = group_image(2 * pairs - 2), group_image(2 * pairs - 1)

    for off in range(1, strips):
        source = lax.rem(me + off, strips)
        pltpu.make_async_remote_copy(
            src_ref=outbox.at[me], dst_ref=inbox.at[source],
            send_sem=s_send.at[me], recv_sem=s_recv.at[source],
            device_id=(v, source), device_id_type=MESH,
        ).wait_recv()
    arrived = inbox[...].reshape(strips * TILE, piece)
    spread = spread_ref[...]
    science = []
    for f in range(fold):
        mine = pltpu.roll(spread, f * capacity, 1) if f else spread
        science.append(jnp.dot(mine.astype(BF16), arrived, preferred_element_type=F32))
    science = jnp.concatenate(science, axis=1)
    upper, middle, lower = split_three(science)
    which = lax.broadcasted_iota(jnp.int32, science.shape, 0) % GROUP
    spare = basis_count % GROUP
    second = jnp.where(which == spare, upper, second)
    second = jnp.where(which == spare + 1, middle, second)
    second = jnp.where(which == spare + 2, lower, second)
    put(pairs - 1, first, second)

    def gram_step(r, total):
        image = images[r]
        return total + lax.dot_general(
            image, image, (((1,), (1,)), ((), ())), preferred_element_type=F32
        )

    gram = lax.fori_loop(0, rows, gram_step, jnp.zeros((padded, padded), F32), unroll=4)

    my_low = lax.rem(me, low)
    my_high = me // low
    low_buf[my_low] = jnp.zeros((padded, LANES), F32)
    low_buf[my_low, :, 0:padded] = gram

    def low_copy(slot_id, peer):
        return pltpu.make_async_remote_copy(
            src_ref=low_buf.at[slot_id], dst_ref=low_buf.at[slot_id],
            send_sem=low_send.at[peer], recv_sem=low_recv.at[slot_id],
            device_id=(v, my_high * low + peer), device_id_type=MESH,
        )

    def high_copy(slot_id, peer):
        return pltpu.make_async_remote_copy(
            src_ref=high_buf.at[slot_id], dst_ref=high_buf.at[slot_id],
            send_sem=high_send.at[peer], recv_sem=high_recv.at[slot_id],
            device_id=(v, peer * low + my_low), device_id_type=MESH,
        )

    for off in range(1, low):
        low_copy(my_low, lax.rem(my_low + off, low)).start()
    for off in range(1, low):
        peer = lax.rem(my_low + off, low)
        low_copy(peer, peer).wait_recv()
    high_buf[my_high] = jnp.sum(low_buf[...], axis=0)
    for off in range(1, high):
        high_copy(my_high, lax.rem(my_high + off, high)).start()
    for off in range(1, high):
        peer = lax.rem(my_high + off, high)
        high_copy(peer, peer).wait_recv()
    system = jnp.sum(high_buf[...], axis=0)

    rhs = basis_count
    lane = lax.broadcasted_iota(jnp.int32, (padded, LANES), 1)
    sub = lax.broadcasted_iota(jnp.int32, (padded, LANES), 0)
    moment = (
        system[:, rhs : rhs + 1] + system[:, rhs + 1 : rhs + 2] + system[:, rhs + 2 : rhs + 3]
    )
    system = jnp.where(lane == rhs, moment, system)
    for j in range(basis_count):
        pivot = system[j : j + 1, :] / system[j : j + 1, j : j + 1]
        column = jnp.where(sub == j, 0.0, system[:, j : j + 1])
        system = jnp.where(sub == j, pivot, system - column * pivot)
    answer = jnp.where((sub == lane) & (sub < basis_count), system[:, rhs : rhs + 1], 0.0)
    answer = jnp.sum(answer, axis=0, keepdims=True)
    coef_ref[...] = answer[:, 0:basis_count]

    upper, middle, lower = split_three(-answer)
    lane8 = lax.broadcasted_iota(jnp.int32, (GROUP, LANES), 1)
    upper = jnp.where((lane8[0:1] >= rhs) & (lane8[0:1] < rhs + 3), 1.0, upper)
    weights = jnp.where(line == 0, upper, jnp.where(line == 1, middle, jnp.where(line == 2, lower, 0.0)))
    weights = weights[:, 0:padded].astype(BF16)
    for r in range(rows):
        model = jnp.dot(weights, images[r], preferred_element_type=F32)
        diff_ref[r : r + 1, :] = jnp.sum(model, axis=0, keepdims=True)

    for off in range(visits):
        to = lax.rem(v + off, visits)
        if off:
            main_copy(v, to).wait_send()

        @pl.when(me < strips - 1)
        def _():
            down_copy(v, to, me + 1).wait_send()

        @pl.when(me > 0)
        def _():
            up_copy(v, to, me - 1).wait_send()

    for off in range(1, strips):
        row_copy(off).wait_send()
    for off in range(1, low):
        low_copy(my_low, lax.rem(my_low + off, low)).wait_send()
    for off in range(1, high):
        high_copy(my_high, lax.rem(my_high + off, high)).wait_send()


def body(template, science_src, target_rows, row_taps, col_taps):
    basis_count = row_taps.shape[0]
    strips = lax.axis_size("strip")
    visits = lax.axis_size("visit")
    rows_dev, part_width = template.shape
    full_width = part_width * visits
    src_dev = science_src.shape[1]
    capacity = max(2, 2 * src_dev // strips)
    fold = TILE // capacity
    piece = full_width // fold
    padded = (basis_count + 3 + TILE - 1) // TILE * TILE
    height = rows_dev + 2 * TILE
    low = 2 ** (int(math.log2(strips)) // 2)
    high = strips // low
    my_strip = lax.axis_index("strip")
    targets = target_rows[0].reshape(strips, src_dev)
    dest_strip = targets // rows_dev
    row_order = jnp.arange(src_dev, dtype=jnp.int32)
    shared_dest = (dest_strip[:, :, None] == dest_strip[:, None, :]) & (
        row_order[:, None] < row_order[None, :]
    )[None]
    arrival = jnp.sum(shared_dest.astype(jnp.int32), axis=1)
    place = lax.dynamic_slice_in_dim(dest_strip * TILE + arrival, my_strip, 1, 0)
    slot_ids = jnp.arange(strips * TILE, dtype=jnp.int32)
    anchor = (jnp.arange(strips, dtype=jnp.int32) * TILE)[:, None] + arrival
    aimed_here = dest_strip == my_strip
    local_row = targets - my_strip * rows_dev
    slot_hit = (aimed_here[..., None] & (anchor[..., None] == slot_ids)).reshape(
        strips * src_dev, strips * TILE
    )
    line_rows = jnp.arange(rows_dev * GROUP, dtype=jnp.int32) // GROUP
    row_hit = (local_row[..., None] == line_rows).reshape(strips * src_dev, rows_dev * GROUP)
    spread = lax.dot_general(
        row_hit.astype(BF16), slot_hit.astype(BF16), (((0,), (0,)), ((), ())),
        preferred_element_type=F32,
    )
    vmem = pl.BlockSpec(memory_space=pltpu.VMEM)
    dma = pltpu.SemaphoreType.DMA
    difference, coeffs = pl.pallas_call(
        functools.partial(fit_kernel, (visits, strips, capacity, low, high)),
        out_shape=(
            jax.ShapeDtypeStruct((rows_dev, full_width), F32),
            jax.ShapeDtypeStruct((1, basis_count), F32),
        ),
        in_specs=[vmem] * 6,
        out_specs=(vmem, vmem),
        scratch_shapes=[
            pltpu.VMEM((height, full_width), BF16),
            pltpu.VMEM((strips, TILE, piece), BF16),
            pltpu.VMEM((strips, TILE, piece), BF16),
            pltpu.VMEM((full_width // LANES * height, 2 * LANES), BF16),
            pltpu.VMEM((2, padded, LANES), F32),
            pltpu.VMEM((padded, TILE, LANES), F32),
            pltpu.VMEM((2 * LANES, padded * LANES), BF16),
            pltpu.VMEM((padded // GROUP, rows_dev * GROUP, GROUP * height), BF16),
            pltpu.VMEM((2, GROUP * height, full_width), BF16),
            pltpu.VMEM((rows_dev, padded, full_width), BF16),
            pltpu.VMEM((low, padded, LANES), F32),
            pltpu.VMEM((high, padded, LANES), F32),
            dma((3, visits)),
            dma((3, visits)),
            dma((strips,)),
            dma((strips,)),
            dma((low,)),
            dma((low,)),
            dma((high,)),
            dma((high,)),
        ],
        compiler_params=pltpu.CompilerParams(
            collective_id=0, has_side_effects=True, vmem_limit_bytes=50 * 1024 * 1024
        ),
    )(template, science_src[0], place, spread, row_taps, col_taps)
    return (difference[None], coeffs)


def solution(mesh):
    in_specs = (P("strip", "visit"), P("visit", "strip", None), P("visit", None), P(), P())
    out_specs = (P("visit", "strip", None), P("visit", None))
    return jax.shard_map(body, mesh=mesh, in_specs=in_specs, out_specs=out_specs, check_vma=False)
```

time: 162 us -> 34.7 us (0.21)
  blocking collectives: 65.5 us -> 0 us
  other arithmetic: 40.5 us -> 1 us
  Pallas kernels: 0 us -> 28.5 us
  matrix products: 27.5 us -> 0.92 us
  starting transfers between devices: 13 us -> 0 us
  local copies, waits for them, and re-layouts: 13.5 us -> 3.31 us
    psum x1 -> x0, blocking collectives: 60.7 us -> none  [body(): gram_total, moment = lax.psum((gram_part, moment_part), 'strip')]
    pallas_call x0 -> x1, Pallas kernels: none -> 28.5 us  [body(): pl.pallas_call(functools.partial(fit_kernel, (visits, strips, capacity, l...]
    dot_general x7 -> x1, matrix products: 27.2 us -> 0.92 us  [body(): lax.dot_general(row_hit.astype(BF16), slot_hit.astype(BF16), (((0,), (0,)...]
    convert_element_type x7 -> x0, other arithmetic: 17.6 us -> none  [the longest x1 11.5 us: convolve(): band_table.astype(jnp.bfloat16)]
    eq x23 -> x0, other arithmetic: 9.67 us -> none  [the longest x11 6.85 us: convolve(): row_lag == t]
    all_to_all x1 -> x0, starting transfers between devices: 9.35 us -> none  [body(): lax.all_to_all(outgoing, 'strip', split_axis=0, concat_axis=0, tiled=True)]
    another operation x7 -> x0, other arithmetic: 8.9 us -> none  [the longest x3 4.78 us: body(): factor = jnp.linalg.cholesky(gram_total)]
    reshape x3 -> x0, local copies, waits for them, and re-layouts: 8.63 us -> none  [the longest x1 8.52 us: convolve(): jnp.transpose(smoothed, (2, 0, 1, 3))]
  transfers between devices with their start and end apart: 3 -> 0, of which waited for: 0 -> 0; matrix products, arithmetic and copies ran while one was open for 41% -> 0% of each run, Pallas kernels for 0% -> 0%
where the time goes in v1:
time: 34.7 us; the launch traced here: 34.5 us
  Pallas kernels  28.5 us (82%)
  local copies, waits for them, and re-layouts  3.31 us (10%)
  other arithmetic  1 us (3%)
  matrix products  0.92 us (3%)
  between operations  0.73 us (2%)
    pallas_call x1, Pallas kernels, body(): pl.pallas_call(functools.partial(fit_kernel, (visits, strips, capacity, l...  28.5 us
    unnamed x15, local copies, waits for them, and re-layouts  3.24 us
    dot_general x1, matrix products, body(): lax.dot_general(row_hit.astype(BF16), slot_hit.astype(BF16), (((0,), (0,)...  0.92 us

profile of v1, /device:TPU:0, one launch (start us, length us, event | category | flops | bytes accessed | tf_op | source)
XLA Modules:
  0.0 34.5 jit_solution(1254747943359812675)
XLA Ops:
  0.6 0.0 copy-start.4
  0.7 0.5 %broadcast.143 = s32[]{:T(128)} broadcast(s32[]{:T(128)} %constant.32.clone.1), dimensions={} | broadcast | bytes 8 | tf_op args[2]
  1.2 0.1 copy-done.4
  1.3 0.7 %reduce.3 = s32[1024]{0:T(1024)S(1)} reduce(s32[1,1024]{1,0:T(1,128)S(1)} %copy-done.4, s32[]{:T(128)} %broadcast.143), dimensions={0}, to_apply=%param.7.reduce_sub_computation.3 | reduce | bytes 8196 | tf_op args[2]
  2.0 0.1 reshape_squeeze.3
  2.1 0.2 convert_reduce_fusion
  2.3 0.0 copy-start.2
  2.3 0.1 broadcast_add_fusion
  2.4 0.6 %copy-done.2 = bf16[45,21]{0,1:T(8,128)(2,1)S(1)} copy-done((bf16[45,21]{0,1:T(8,128)(2,1)S(1)}, bf16[45,21]{0,1:T(8,128)(2,1)}, u32[]{:S(2)}) %copy-start.2) | copy-done | bytes 1914
  3.0 0.0 copy-start.3
  3.0 0.1 copy.9.row_ref
  3.1 0.6 %copy-done.3 = bf16[45,21]{0,1:T(8,128)(2,1)S(1)} copy-done((bf16[45,21]{0,1:T(8,128)(2,1)S(1)}, bf16[45,21]{0,1:T(8,128)(2,1)}, u32[]{:S(2)}) %copy-start.3) | copy-done | bytes 1914
  3.7 0.1 copy.10.col_ref
  3.8 0.0 copy-start
  3.8 0.0 copy-start.1
  3.8 0.9 %convolution_bitcast_fusion.spread_ref = f32[256,256]{1,0:T(8,128)S(1)} fusion(s32[16,64]{1,0:T(8,128)S(1)} %get-tuple-element.8, s32[256]{0:T(256)S(1)} %and_select_fusion, s32[16,64]{1,0:T(8,128)S(1)} %get-tuple-element.9, pred[16,64]{1,0:T(8,128)(4,1)S(1)} %get-tuple-element.6), kind=kOutput, calls=%fused_computation | convolution fusion | flops 135004160 | bytes 272384 | tf_op jit(solution)/shard_map/dot_general | solution.py:362
  4.8 0.0 copy-done
  4.8 0.0 copy-done.1
  4.8 28.5 %shard_map.68 = (f32[32,1024]{1,0:T(8,128)S(1)}, f32[1,45]{1,0:T(1,128)S(1)}) custom-call(bf16[32,512]{1,0:T(8,128)(2,1)S(1)} %copy-done.1, bf16[64,1024]{1,0:T(8,128)(2,1)S(1)} %bitcast.5, s32[1,64]{1,0:T(1,128)S(1)} %dynamic-slice_add_fusion.place_ref, f32[256,256]{1,0:T(8,128)S(1)} %convolution_bitcast_fusion.spread_ref, bf16[45,21]{1,0:T(8,128)(2,1)S(1)} %copy.9.row_ref, ...), custom_call_target="tpu_custom_call" | custom-call | tf_op jit(solution)/shard_map/pallas_call | solution.py:368
  33.3 0.7 %copy.13 = f32[1,32,1024]{2,1,0:T(8,128)} copy(f32[1,32,1024]{2,1,0:T(8,128)S(1)} %bitcast.4) | data formatting | bytes 262144
  34.0 0.5 %copy.14 = f32[1,45]{1,0:T(1,128)} copy(f32[1,45]{1,0:T(1,128)S(1)} %get-tuple-element.13) | data formatting | bytes 360
  (5 shorter events, 0.0 us)
Async XLA Ops:
  0.6 0.7 %copy-start.4 = (s32[1,1024]{1,0:T(1,128)S(1)}, s32[1,1024]{1,0:T(1,128)}, u32[]{:S(2)}) copy-start(s32[1,1024]{1,0:T(1,128)} %param.7) | copy-start | bytes 12292
  2.3 0.7 %copy-start.2 = (bf16[45,21]{0,1:T(8,128)(2,1)S(1)}, bf16[45,21]{0,1:T(8,128)(2,1)}, u32[]{:S(2)}) copy-start(bf16[45,21]{0,1:T(8,128)(2,1)} %param.8) | copy-start | bytes 5674
  3.0 0.7 %copy-start.3 = (bf16[45,21]{0,1:T(8,128)(2,1)S(1)}, bf16[45,21]{0,1:T(8,128)(2,1)}, u32[]{:S(2)}) copy-start(bf16[45,21]{0,1:T(8,128)(2,1)} %param.9) | copy-start | bytes 5674
  3.8 0.9 %copy-start = (bf16[1,64,1024]{2,1,0:T(8,128)(2,1)S(1)}, bf16[1,64,1024]{2,1,0:T(8,128)(2,1)}, u32[]{:S(2)}) copy-start(bf16[1,64,1024]{2,1,0:T(8,128)(2,1)} %param.6) | copy-start | bytes 393220
  3.8 0.9 %copy-start.1 = (bf16[32,512]{1,0:T(8,128)(2,1)S(1)}, bf16[32,512]{1,0:T(8,128)(2,1)}, u32[]{:S(2)}) copy-start(bf16[32,512]{1,0:T(8,128)(2,1)} %tmpl_ref.1) | copy-start | bytes 98308

commit v2 on v1

--- a/solution.py
+++ b/solution.py
@@ -25,10 +25,11 @@
 
 def fit_kernel(
     dims,
-    tmpl_ref, src_ref, place_ref, spread_ref, row_ref, col_ref,
+    tmpl_ref, src_ref, target_ref, row_ref, col_ref,
     diff_ref, coef_ref,
-    frame, outbox, inbox, wide, taps_pad, lag, band, rowband, sm, images, low_buf, high_buf,
+    frame, outbox, inbox, wide, taps_pad, lag, band, rowband, sm, images, science, low_buf, high_buf, rhs_buf,
     t_send, t_recv, s_send, s_recv, low_send, low_recv, high_send, high_recv,
+    rhs_send, rhs_recv,
 ):
     visits, strips, capacity, low, high = dims
     v = lax.axis_index("visit")
@@ -62,10 +63,20 @@
         def _():
             pl.semaphore_signal(barrier, inc=1, device_id=(other, me + 1), device_id_type=MESH)
 
-    slot = lax.broadcasted_iota(jnp.int32, (strips * TILE, src_ref.shape[0]), 0)
+    src_dev = src_ref.shape[0]
+    row_bits = int(math.log2(rows))
+    earlier = (
+        lax.broadcasted_iota(jnp.int32, (src_dev, src_dev), 0)
+        < lax.broadcasted_iota(jnp.int32, (src_dev, src_dev), 1)
+    ).astype(F32).astype(BF16)
+    aim = lax.shift_right_logical(target_ref[pl.ds(me, 1), :], row_bits)
+    hits = (lax.broadcasted_iota(jnp.int32, (strips, src_dev), 0) == aim).astype(F32)
+    ahead = jnp.dot(hits.astype(BF16), earlier, preferred_element_type=F32)
+    place = aim.astype(F32) * TILE + jnp.sum(hits * ahead, axis=0, keepdims=True)
+    slot = lax.broadcasted_iota(jnp.int32, (strips * TILE, src_dev), 0).astype(F32)
     packed = jnp.zeros((strips * TILE, piece), F32)
     for f in range(fold):
-        hit = (slot == place_ref[...] + f * capacity).astype(F32).astype(BF16)
+        hit = (slot == place + float(f * capacity)).astype(F32).astype(BF16)
         packed += jnp.dot(
             hit, src_ref[:, f * piece : (f + 1) * piece], preferred_element_type=F32
         )
@@ -113,16 +124,23 @@
         def _():
             up_copy(v, to, me - 1).start()
 
-    def row_copy(off):
-        to = lax.rem(me + off, strips)
+    def partner(mask):
+        to = me
+        for bit in range(int(math.log2(strips))):
+            if mask >> bit & 1:
+                to = to + 2**bit * (1 - 2 * lax.rem(me // 2**bit, 2))
+        return to
+
+    def row_copy(mask):
+        to = partner(mask)
         return pltpu.make_async_remote_copy(
             src_ref=outbox.at[to], dst_ref=inbox.at[me],
             send_sem=s_send.at[to], recv_sem=s_recv.at[me],
             device_id=(v, to), device_id_type=MESH,
         )
 
-    for off in range(1, strips):
-        row_copy(off).start()
+    for mask in range(strips - 1, 0, -1):
+        row_copy(mask).start()
 
     inbox[me] = outbox[me]
     frame[pl.ds(TILE, rows), span(v)] = tmpl_ref[...]
@@ -178,6 +196,21 @@
                 )
             rowband[g, r * GROUP : (r + 2) * GROUP, :] = jnp.concatenate(pair, axis=0).astype(BF16)
 
+    targets = target_ref[...]
+    mine = lax.shift_right_logical(targets, row_bits) == me
+    order = jnp.dot(mine.astype(F32).astype(BF16), earlier, preferred_element_type=F32)
+    order = jnp.where(mine, order, -1.0)
+    goal = (targets - me * rows + 1).astype(F32)
+    place3 = lax.broadcasted_iota(jnp.int32, (strips, TILE, src_dev), 1).astype(F32)
+    line_row = (lax.broadcasted_iota(jnp.int32, (strips * TILE, rows * GROUP), 1) // GROUP).astype(F32)
+    landing = []
+    for f in range(fold):
+        taken = (place3 - float(f * capacity)) == order[:, None, :]
+        found = jnp.where(taken & (place3 >= float(f * capacity)), goal[:, None, :], 0.0)
+        found = found.reshape(strips * TILE, src_dev)
+        found = jnp.sum(found, axis=1, keepdims=True)
+        landing.append((found == line_row + 1.0).astype(F32).astype(BF16))
+
     for off in range(1, visits):
         main_copy(lax.rem(v + off, visits), v).wait_recv()
     for off in range(visits):
@@ -216,31 +249,8 @@
         ).astype(BF16)
 
     pairs = padded // TILE
-    for pair in range(pairs - 1):
+    for pair in range(pairs):
         put(pair, group_image(2 * pair), group_image(2 * pair + 1))
-    first, second = group_image(2 * pairs - 2), group_image(2 * pairs - 1)
-
-    for off in range(1, strips):
-        source = lax.rem(me + off, strips)
-        pltpu.make_async_remote_copy(
-            src_ref=outbox.at[me], dst_ref=inbox.at[source],
-            send_sem=s_send.at[me], recv_sem=s_recv.at[source],
-            device_id=(v, source), device_id_type=MESH,
-        ).wait_recv()
-    arrived = inbox[...].reshape(strips * TILE, piece)
-    spread = spread_ref[...]
-    science = []
-    for f in range(fold):
-        mine = pltpu.roll(spread, f * capacity, 1) if f else spread
-        science.append(jnp.dot(mine.astype(BF16), arrived, preferred_element_type=F32))
-    science = jnp.concatenate(science, axis=1)
-    upper, middle, lower = split_three(science)
-    which = lax.broadcasted_iota(jnp.int32, science.shape, 0) % GROUP
-    spare = basis_count % GROUP
-    second = jnp.where(which == spare, upper, second)
-    second = jnp.where(which == spare + 1, middle, second)
-    second = jnp.where(which == spare + 2, lower, second)
-    put(pairs - 1, first, second)
 
     def gram_step(r, total):
         image = images[r]
@@ -252,8 +262,10 @@
 
     my_low = lax.rem(me, low)
     my_high = me // low
-    low_buf[my_low] = jnp.zeros((padded, LANES), F32)
-    low_buf[my_low, :, 0:padded] = gram
+    half = padded // 2
+    low_buf[my_low] = jnp.zeros((half, LANES), F32)
+    low_buf[my_low, :, 0:padded] = gram[0:half]
+    low_buf[my_low, :, lead : lead + padded] = gram[half:padded]
 
     def low_copy(slot_id, peer):
         return pltpu.make_async_remote_copy(
@@ -277,34 +289,79 @@
     high_buf[my_high] = jnp.sum(low_buf[...], axis=0)
     for off in range(1, high):
         high_copy(my_high, lax.rem(my_high + off, high)).start()
+    for mask in range(strips - 1, 0, -1):
+        source = partner(mask)
+        pltpu.make_async_remote_copy(
+            src_ref=outbox.at[me], dst_ref=inbox.at[source],
+            send_sem=s_send.at[me], recv_sem=s_recv.at[source],
+            device_id=(v, source), device_id_type=MESH,
+        ).wait_recv()
+    arrived = inbox[...].reshape(strips * TILE, piece)
+    for f in range(fold):
+        science[:, :, f * piece : (f + 1) * piece] = lax.dot_general(
+            landing[f], arrived, (((0,), (0,)), ((), ())), preferred_element_type=F32
+        ).reshape(rows, GROUP, piece)
+
+    bands = padded // GROUP
+
+    def moment_step(r, total):
+        for b in range(blocks):
+            cells = images[r, :, b * LANES : (b + 1) * LANES].astype(F32)
+            total = total + cells.reshape(bands, GROUP, LANES) * science[
+                r, :, b * LANES : (b + 1) * LANES
+            ][None]
+        return total
+
+    products = lax.fori_loop(0, rows, moment_step, jnp.zeros((bands, GROUP, LANES), F32), unroll=2)
+    lane = lax.broadcasted_iota(jnp.int32, (padded, LANES), 1)
+    sub = lax.broadcasted_iota(jnp.int32, (padded, LANES), 0)
+    moment = jnp.sum(products.reshape(padded, LANES), axis=1, keepdims=True)
+    moment = jnp.sum(jnp.where(sub == lane, moment, 0.0), axis=0, keepdims=True)
+    rhs_buf[me] = jnp.where(line == 0, moment, 0.0)
+
+    def rhs_copy(mask):
+        to = partner(mask)
+        return pltpu.make_async_remote_copy(
+            src_ref=rhs_buf.at[me], dst_ref=rhs_buf.at[me],
+            send_sem=rhs_send.at[to], recv_sem=rhs_recv.at[me],
+            device_id=(v, to), device_id_type=MESH,
+        )
+
+    for mask in range(strips - 1, 0, -1):
+        rhs_copy(mask).start()
+
     for off in range(1, high):
         peer = lax.rem(my_high + off, high)
         high_copy(peer, peer).wait_recv()
-    system = jnp.sum(high_buf[...], axis=0)
-
-    rhs = basis_count
-    lane = lax.broadcasted_iota(jnp.int32, (padded, LANES), 1)
-    sub = lax.broadcasted_iota(jnp.int32, (padded, LANES), 0)
-    moment = (
-        system[:, rhs : rhs + 1] + system[:, rhs + 1 : rhs + 2] + system[:, rhs + 2 : rhs + 3]
-    )
-    system = jnp.where(lane == rhs, moment, system)
+    halves = jnp.sum(high_buf[...], axis=0)
+
+    system = jnp.concatenate([halves, pltpu.roll(halves, lead, 1)], axis=0)
+    system = jnp.where(lane < lead, system, (lane - lead == sub).astype(F32))
     for j in range(basis_count):
         pivot = system[j : j + 1, :] / system[j : j + 1, j : j + 1]
         column = jnp.where(sub == j, 0.0, system[:, j : j + 1])
         system = jnp.where(sub == j, pivot, system - column * pivot)
-    answer = jnp.where((sub == lane) & (sub < basis_count), system[:, rhs : rhs + 1], 0.0)
-    answer = jnp.sum(answer, axis=0, keepdims=True)
+    inverse = pltpu.roll(system, lead, 1)
+    inverse = jnp.where((lane < basis_count) & (sub < basis_count), inverse, 0.0)
+
+    for mask in range(strips - 1, 0, -1):
+        source = partner(mask)
+        pltpu.make_async_remote_copy(
+            src_ref=rhs_buf.at[me], dst_ref=rhs_buf.at[source],
+            send_sem=rhs_send.at[me], recv_sem=rhs_recv.at[source],
+            device_id=(v, source), device_id_type=MESH,
+        ).wait_recv()
+    moment = jnp.sum(jnp.sum(rhs_buf[...], axis=0), axis=0, keepdims=True)
+    answer = jnp.sum(inverse * moment, axis=1, keepdims=True)
+    answer = jnp.sum(jnp.where(sub == lane, answer, 0.0), axis=0, keepdims=True)
     coef_ref[...] = answer[:, 0:basis_count]
 
     upper, middle, lower = split_three(-answer)
-    lane8 = lax.broadcasted_iota(jnp.int32, (GROUP, LANES), 1)
-    upper = jnp.where((lane8[0:1] >= rhs) & (lane8[0:1] < rhs + 3), 1.0, upper)
     weights = jnp.where(line == 0, upper, jnp.where(line == 1, middle, jnp.where(line == 2, lower, 0.0)))
     weights = weights[:, 0:padded].astype(BF16)
     for r in range(rows):
         model = jnp.dot(weights, images[r], preferred_element_type=F32)
-        diff_ref[r : r + 1, :] = jnp.sum(model, axis=0, keepdims=True)
+        diff_ref[r : r + 1, :] = science[r, 0:1, :] + jnp.sum(model, axis=0, keepdims=True)
 
     for off in range(visits):
         to = lax.rem(v + off, visits)
@@ -319,8 +376,9 @@
         def _():
             up_copy(v, to, me - 1).wait_send()
 
-    for off in range(1, strips):
-        row_copy(off).wait_send()
+    for mask in range(strips - 1, 0, -1):
+        row_copy(mask).wait_send()
+        rhs_copy(mask).wait_send()
     for off in range(1, low):
         low_copy(my_low, lax.rem(my_low + off, low)).wait_send()
     for off in range(1, high):
@@ -337,32 +395,11 @@
     capacity = max(2, 2 * src_dev // strips)
     fold = TILE // capacity
     piece = full_width // fold
-    padded = (basis_count + 3 + TILE - 1) // TILE * TILE
+    padded = (basis_count + TILE - 1) // TILE * TILE
     height = rows_dev + 2 * TILE
     low = 2 ** (int(math.log2(strips)) // 2)
     high = strips // low
-    my_strip = lax.axis_index("strip")
     targets = target_rows[0].reshape(strips, src_dev)
-    dest_strip = targets // rows_dev
-    row_order = jnp.arange(src_dev, dtype=jnp.int32)
-    shared_dest = (dest_strip[:, :, None] == dest_strip[:, None, :]) & (
-        row_order[:, None] < row_order[None, :]
-    )[None]
-    arrival = jnp.sum(shared_dest.astype(jnp.int32), axis=1)
-    place = lax.dynamic_slice_in_dim(dest_strip * TILE + arrival, my_strip, 1, 0)
-    slot_ids = jnp.arange(strips * TILE, dtype=jnp.int32)
-    anchor = (jnp.arange(strips, dtype=jnp.int32) * TILE)[:, None] + arrival
-    aimed_here = dest_strip == my_strip
-    local_row = targets - my_strip * rows_dev
-    slot_hit = (aimed_here[..., None] & (anchor[..., None] == slot_ids)).reshape(
-        strips * src_dev, strips * TILE
-    )
-    line_rows = jnp.arange(rows_dev * GROUP, dtype=jnp.int32) // GROUP
-    row_hit = (local_row[..., None] == line_rows).reshape(strips * src_dev, rows_dev * GROUP)
-    spread = lax.dot_general(
-        row_hit.astype(BF16), slot_hit.astype(BF16), (((0,), (0,)), ((), ())),
-        preferred_element_type=F32,
-    )
     vmem = pl.BlockSpec(memory_space=pltpu.VMEM)
     dma = pltpu.SemaphoreType.DMA
     difference, coeffs = pl.pallas_call(
@@ -371,7 +408,7 @@
             jax.ShapeDtypeStruct((rows_dev, full_width), F32),
             jax.ShapeDtypeStruct((1, basis_count), F32),
         ),
-        in_specs=[vmem] * 6,
+        in_specs=[vmem] * 5,
         out_specs=(vmem, vmem),
         scratch_shapes=[
             pltpu.VMEM((height, full_width), BF16),
@@ -384,8 +421,10 @@
             pltpu.VMEM((padded // GROUP, rows_dev * GROUP, GROUP * height), BF16),
             pltpu.VMEM((2, GROUP * height, full_width), BF16),
             pltpu.VMEM((rows_dev, padded, full_width), BF16),
-            pltpu.VMEM((low, padded, LANES), F32),
-            pltpu.VMEM((high, padded, LANES), F32),
+            pltpu.VMEM((rows_dev, GROUP, full_width), F32),
+            pltpu.VMEM((low, padded // 2, LANES), F32),
+            pltpu.VMEM((high, padded // 2, LANES), F32),
+            pltpu.VMEM((strips, GROUP, LANES), F32),
             dma((3, visits)),
             dma((3, visits)),
             dma((strips,)),
@@ -394,11 +433,13 @@
             dma((low,)),
             dma((high,)),
             dma((high,)),
+            dma((strips,)),
+            dma((strips,)),
         ],
         compiler_params=pltpu.CompilerParams(
             collective_id=0, has_side_effects=True, vmem_limit_bytes=50 * 1024 * 1024
         ),
-    )(template, science_src[0], place, spread, row_taps, col_taps)
+    )(template, science_src[0], targets, row_taps, col_taps)
     return (difference[None], coeffs)
 
 

time: 34.7 us -> 33.6 us (0.968)
  matrix products: 0.92 us -> 0 us
  Pallas kernels: 28.5 us -> 27.8 us
  other arithmetic: 1 us -> 1.35 us
    dot_general x1 -> x0, matrix products: 0.92 us -> none  [body(): lax.dot_general(row_hit.astype(BF16), slot_hit.astype(BF16), (((0,), (0,)...]
    pallas_call x1, Pallas kernels: 28.5 us -> 27.8 us  [body(): pl.pallas_call(functools.partial(fit_kernel, (visits, strips, capacity, l...]
    unnamed x1, other arithmetic: 0.66 us -> 1.35 us
    unnamed x15 -> x11, local copies, waits for them, and re-layouts: 3.24 us -> 3.51 us
where the time goes in v2:
time: 33.6 us; the launch traced here: 33.4 us
  Pallas kernels  27.8 us (83%)
  local copies, waits for them, and re-layouts  3.58 us (11%)
  other arithmetic  1.35 us (4%)
  between operations  0.66 us (2%)
    pallas_call x1, Pallas kernels, body(): pl.pallas_call(functools.partial(fit_kernel, (visits, strips, capacity, l...  27.8 us
    unnamed x11, local copies, waits for them, and re-layouts  3.51 us
    unnamed x1, other arithmetic  1.35 us

profile of v2, /device:TPU:0, one launch (start us, length us, event | category | flops | bytes accessed | tf_op | source)
XLA Modules:
  0.0 33.4 jit_solution(9726051527857073245)
XLA Ops:
  0.6 0.0 copy-start.1
  0.6 0.5 %broadcast.3 = s32[]{:T(128)} broadcast(s32[]{:T(128)} %constant.5), dimensions={} | broadcast | bytes 8 | tf_op args[2]
  1.2 1.3 %reduce.3 = s32[1024]{0:T(1024)S(1)} reduce(s32[1,1024]{1,0:T(1,128)} %param.7, s32[]{:T(128)} %broadcast.3), dimensions={0}, to_apply=%param.7.reduce_sub_computation.3 | reduce | bytes 8196 | tf_op args[2]
  2.5 0.1 reshape_squeeze.3.target_ref
  2.6 0.0 copy-start.2
  2.6 0.8 %copy.7.row_ref = bf16[45,21]{1,0:T(8,128)(2,1)S(1)} copy(bf16[45,21]{0,1:T(8,128)(2,1)} %param.8) | data formatting | bytes 3780 | tf_op args[3]
  3.4 0.0 copy-done.2
  3.4 0.1 copy.8.col_ref
  3.5 0.0 copy-done.1
  3.5 0.0 copy-start
  3.5 0.9 %copy-done = bf16[1,64,1024]{2,1,0:T(8,128)(2,1)S(1)} copy-done((bf16[1,64,1024]{2,1,0:T(8,128)(2,1)S(1)}, bf16[1,64,1024]{2,1,0:T(8,128)(2,1)}, u32[]{:S(2)}) %copy-start) | copy-done | bytes 131096
  4.4 27.8 %shard_map.68 = (f32[32,1024]{1,0:T(8,128)S(1)}, f32[1,45]{1,0:T(1,128)S(1)}) custom-call(bf16[32,512]{1,0:T(8,128)(2,1)S(1)} %copy-done.1, bf16[64,1024]{1,0:T(8,128)(2,1)S(1)} %bitcast.2, s32[16,64]{1,0:T(8,128)S(1)} %reshape_squeeze.3.target_ref, bf16[45,21]{1,0:T(8,128)(2,1)S(1)} %copy.7.row_ref, bf16[45,21]{1,0:T(8,128)(2,1)S(1)} %copy.8.col_ref), custom_call_target="tpu_custom_call" | custom-call | tf_op jit(solution)/shard_map/pallas_call | solution.py:405
  32.2 0.7 %copy.11 = f32[1,32,1024]{2,1,0:T(8,128)} copy(f32[1,32,1024]{2,1,0:T(8,128)S(1)} %bitcast.3) | data formatting | bytes 262144
  32.9 0.5 %copy.12 = f32[1,45]{1,0:T(1,128)} copy(f32[1,45]{1,0:T(1,128)S(1)} %get-tuple-element.9) | data formatting | bytes 360
Async XLA Ops:
  0.6 2.9 %copy-start.1 = (bf16[32,512]{1,0:T(8,128)(2,1)S(1)}, bf16[32,512]{1,0:T(8,128)(2,1)}, u32[]{:S(2)}) copy-start(bf16[32,512]{1,0:T(8,128)(2,1)} %tmpl_ref.1) | copy-start | bytes 98308
  2.6 0.8 %copy-start.2 = (bf16[45,21]{0,1:T(8,128)(2,1)S(1)}, bf16[45,21]{0,1:T(8,128)(2,1)}, u32[]{:S(2)}) copy-start(bf16[45,21]{0,1:T(8,128)(2,1)} %param.9) | copy-start | bytes 5674
  3.5 0.9 %copy-start = (bf16[1,64,1024]{2,1,0:T(8,128)(2,1)S(1)}, bf16[1,64,1024]{2,1,0:T(8,128)(2,1)}, u32[]{:S(2)}) copy-start(bf16[1,64,1024]{2,1,0:T(8,128)(2,1)} %param.6) | copy-start | bytes 393220
